TPU v7x, 32 devices: a whole 2x2x4 slice. The times are simulated.
32 devices in a mesh: crops: 2 (over y), row: 4 (over x, core), col: 4 (over z).
Axes of the slice: x: 2, y: 2, z: 4, core: 2. Of those that a mesh axis runs over, the one named last changes fastest.
Arguments:
- pair: float32 [192, 96, 128], P(('crops', 'row'), 'col'), parts along dimension 0, may hold values from -6 to 6
- pair_mask: int32 [192, 96], P(('crops', 'row'), 'col'), parts along dimension 0, may hold values 0 or 1
- chain_ids: int32 [192], P('crops'), parts along dimension 0, may hold values from 0 to 3, never falling along the last dimension, each value on 1 to 48 neighbouring positions
- chain_pair_table: float32 [2, 128], replicated, may hold values from -4 to 4
- norms: float32 [2, 4, 128], replicated, may hold values from 0.1 to 1.9
- w_in: bfloat16 [2, 128, 640], replicated, may hold values from -0.5 to 0.5
- w_out: bfloat16 [2, 128, 128], replicated, may hold values from -0.5 to 0.5
Outputs:
- updated: float32 [192, 96, 128], P(('crops', 'row'), 'col'), parts along dimension 0
There are 2 independent parts, one for each index of `crops`. A program takes and returns all parts, laid end to end along the dimension named above; an argument that names none is the same for every part. Nothing has to cross between parts.
Inputs may be any that keep to these rules, and one draw needn't show every extreme that they name: `chain_ids`: chain numbers never fall along the residues; every chain holds one to 48 residues.
All inputs are finite; a program needn't handle non-finite values. No bound on the sum of `pair_mask` on one device may be relied on, other than what follows from the above.
Results may differ from a plain program's by a relative error of at most 0.0023.
Values may be sent and summed in bfloat16 or wider, within the bound.
A program may use at most 64 MiB of HBM per device.

v0:
```python
import jax
import jax.numpy as jnp
from jax import lax
from jax.sharding import PartitionSpec as P


def partner_2(value, axis, distance):
    mask = 2**distance
    pairs = [(source, source ^ mask) for source in range(lax.axis_size(axis))]
    return lax.ppermute(value, axis, pairs)


def layer_norm(value, gain, bias):
    mean = jnp.mean(value, axis=-1, keepdims=True)
    spread = jnp.mean(jnp.square(value - mean), axis=-1, keepdims=True)
    return (value - mean) * lax.rsqrt(spread + 1e-05) * gain + bias


def inputs_of(state, norms_one, weight_in, pair_mask):
    width = state.shape[-1]
    normed = layer_norm(state, norms_one[0], norms_one[1]).astype(jnp.bfloat16)
    projected = jnp.einsum("ijc,cd->ijd", normed, weight_in, preferred_element_type=jnp.float32)
    masking = pair_mask.astype(jnp.float32)[..., None]
    left = (
        masking * jax.nn.sigmoid(projected[..., width : 2 * width]) * projected[..., :width]
    ).astype(jnp.bfloat16)
    right = (
        masking
        * jax.nn.sigmoid(projected[..., 3 * width : 4 * width])
        * projected[..., 2 * width : 3 * width]
    ).astype(jnp.bfloat16)
    gating = jax.nn.sigmoid(projected[..., 4 * width :])
    return (left, right, gating)


def finish(state, triangle, gating, norms_one, weight_out):
    tnorm = layer_norm(triangle, norms_one[2], norms_one[3]).astype(jnp.bfloat16)
    return state + gating * jnp.einsum(
        "ijc,cd->ijd", tnorm, weight_out, preferred_element_type=jnp.float32
    )


def mirrored(block):
    levels = lax.axis_size("col").bit_length() - 1
    row_index = lax.axis_index("row")
    col_index = lax.axis_index("col")
    for level in range(levels):
        moved = block
        for position in (level, level + levels):
            moved = partner_2(moved, ("row", "col"), position)
        differ = row_index >> level & 1 != col_index >> level & 1
        block = jnp.where(differ, moved, block)
    return block


def body(pair, pair_mask, chain_ids, chain_pair_table, norms, w_in, w_out):
    rows_here = pair.shape[0]
    row_start = lax.axis_index("row") * rows_here
    col_start = lax.axis_index("col") * pair.shape[1]
    row_chain = lax.dynamic_slice_in_dim(chain_ids, row_start, rows_here, 0)
    col_chain = lax.dynamic_slice_in_dim(chain_ids, col_start, pair.shape[1], 0)
    same = row_chain[:, None] == col_chain[None, :]
    state = pair + jnp.where(same[..., None], chain_pair_table[1], chain_pair_table[0])
    left, right, gating = inputs_of(state, norms[0], w_in[0], pair_mask)
    partner = mirrored(right)
    right_rows = lax.all_gather(partner, "row", axis=1, tiled=True)
    matching = right_rows
    triangle = jnp.einsum(
        "ikc,jkc->ijc",
        lax.all_gather(left, "col", axis=1, tiled=True),
        matching,
        preferred_element_type=jnp.float32,
    )
    state = finish(state, triangle, gating, norms[0], w_out[0])
    left, right, gating = inputs_of(state, norms[1], w_in[1], pair_mask)
    partner = mirrored(left)
    left_cols = lax.all_gather(partner, "col", axis=0, tiled=True)
    matching = left_cols
    triangle = jnp.einsum(
        "kic,kjc->ijc",
        matching,
        lax.all_gather(right, "row", axis=0, tiled=True),
        preferred_element_type=jnp.float32,
    )
    return finish(state, triangle, gating, norms[1], w_out[1])


def solution(mesh):
    placed = (
        P(("crops", "row"), "col", None),
        P(("crops", "row"), "col"),
        P("crops"),
        P(),
        P(),
        P(),
        P(),
    )
    return jax.shard_map(
        body,
        mesh=mesh,
        in_specs=placed,
        out_specs=P(("crops", "row"), "col", None),
        check_vma=False,
    )
```

profile of v0, /device:TPU:0, one launch (start us, length us, event | category | flops | bytes accessed | tf_op | source)
XLA Modules:
  0.0 120.8 jit_solution(10889917430207526399)
XLA Ops:
  0.0 0.8 slice_bitcast_fusion.9
  0.8 0.9 slice_bitcast_fusion.1
  1.6 0.7 convert_element_type.29
  2.3 0.8 fusion.58
  3.1 0.1 broadcast_compare_fusion
  3.2 1.2 %fusion.28 = f32[24,24]{1,0:T(8,128)S(1)} fusion(f32[24,24,128]{2,1,0:T(8,128)} %param.7, f32[128]{0:T(128)S(1)} %get-tuple-element.18, f32[128]{0:T(128)S(1)} %get-tuple-element.17, pred[24,24]{1,0:T(8,128)(4,1)S(1)} %broadcast_compare_fusion), kind=kLoop, calls=%fused_computation.53 | loop fusion | flops 220608 | bytes 298816 | tf_op jit(solution)/shard_map/reduce_sum | solution.py:14
  4.5 1.3 %multiply_reduce_fusion.3 = f32[24,24]{1,0:T(8,128)S(1)} fusion(f32[24,24,128]{2,1,0:T(8,128)} %param.7, f32[24,24]{1,0:T(8,128)S(1)} %broadcast_multiply_fusion.3, f32[128]{0:T(128)S(1)} %get-tuple-element.18, f32[128]{0:T(128)S(1)} %get-tuple-element.17, pred[24,24]{1,0:T(8,128)(4,1)S(1)} %broadcast_compare_fusion), kind=kLoop, calls=%fused_computation.51 | loop fusion | flops 368064 | bytes 301120 | tf_op jit(solution)/shard_map/reduce_sum | solution.py:15
  5.8 1.6 %fusion.31 = f32[24,24,640]{2,1,0:T(8,128)S(1)} fusion(bf16[2,128,640]{2,1,0:T(8,128)(2,1)} %param.12, f32[24,24,128]{2,1,0:T(8,128)} %param.7, f32[128]{0:T(128)S(1)} %get-tuple-element.14, f32[128]{0:T(128)S(1)} %get-tuple-element.15, f32[24,24]{1,0:T(8,128)S(1)} %add_rsqrt_fusion.3, f32[24,24]{1,0:T(8,128)S(1)} %broadcast_multiply_fusion.3, ...), kind=kOutput, calls=%fused_computation.56 | convolution fusion | flops 94887936 | bytes 1940544 | tf_op jit(solution)/shard_map/ijc,cd->ijd/dot_general | solution.py:22
  7.4 0.2 fusion.15
  7.6 3.1 %collective-permute-start = (bf16[24,24,128]{2,1,0:T(8,128)(2,1)S(1)}, bf16[24,24,128]{2,1,0:T(8,128)(2,1)S(1)}, u32[]{:S(2)}, u32[]{:S(2)}) collective-permute-start(bf16[24,24,128]{2,1,0:T(8,128)(2,1)S(1)} %get-tuple-element.8), channel_id=1, source_target_pairs={{0,1},{1,0},{2,3},{3,2},{4,5},{5,4},{6,7},{7,6},{8,9},{9,8},{10,11... | collective-permute-start | bytes 442376 | tf_op jit(solution)/shard_map/ppermute | solution.py:10
  10.7 3.8 %collective-permute-done = bf16[24,24,128]{2,1,0:T(8,128)(2,1)S(1)} collective-permute-done((bf16[24,24,128]{2,1,0:T(8,128)(2,1)S(1)}, bf16[24,24,128]{2,1,0:T(8,128)(2,1)S(1)}, u32[]{:S(2)}, u32[]{:S(2)}) %collective-permute-start) | collective-permute-done | bytes 147488 | tf_op jit(solution)/shard_map/ppermute | solution.py:10
  14.5 0.0 collective-permute-start.1
  14.5 1.4 %collective-permute-done.1 = bf16[24,24,128]{2,1,0:T(8,128)(2,1)S(1)} collective-permute-done((bf16[24,24,128]{2,1,0:T(8,128)(2,1)S(1)}, bf16[24,24,128]{2,1,0:T(8,128)(2,1)S(1)}, u32[]{:S(2)}, u32[]{:S(2)}) %collective-permute-start.1) | collective-permute-done | bytes 147488 | tf_op jit(solution)/shard_map/ppermute | solution.py:10
  15.9 2.8 %collective-permute-start.2 = (bf16[24,24,128]{2,1,0:T(8,128)(2,1)S(1)}, bf16[24,24,128]{2,1,0:T(8,128)(2,1)S(1)}, u32[]{:S(2)}, u32[]{:S(2)}) collective-permute-start(bf16[24,24,128]{2,1,0:T(8,128)(2,1)S(1)} %broadcast_select_fusion.1), channel_id=1, source_target_pairs={{0,2},{1,3},{2,0},{3,1},{4,6},{5,7},{6,4},{7,5},{8,10},{9,11},{10,... | collective-permute-start | bytes 442376 | tf_op jit(solution)/shard_map/ppermute | solution.py:10
  18.7 7.3 %collective-permute-done.2 = bf16[24,24,128]{2,1,0:T(8,128)(2,1)S(1)} collective-permute-done((bf16[24,24,128]{2,1,0:T(8,128)(2,1)S(1)}, bf16[24,24,128]{2,1,0:T(8,128)(2,1)S(1)}, u32[]{:S(2)}, u32[]{:S(2)}) %collective-permute-start.2) | collective-permute-done | bytes 147488 | tf_op jit(solution)/shard_map/ppermute | solution.py:10
  26.1 1.5 %collective-permute-start.3 = (bf16[24,24,128]{2,1,0:T(8,128)(2,1)S(1)}, bf16[24,24,128]{2,1,0:T(8,128)(2,1)S(1)}, u32[]{:S(2)}, u32[]{:S(2)}) collective-permute-start(bf16[24,24,128]{2,1,0:T(8,128)(2,1)S(1)} %collective-permute-done.2), channel_id=1, source_target_pairs={{0,8},{1,9},{2,10},{3,11},{4,12},{5,13},{6,14},{7,15},{8,0},{9,1},... | collective-permute-start | bytes 442376 | tf_op jit(solution)/shard_map/ppermute | solution.py:10
  27.6 16.8 %all_gather.13 = bf16[24,96,128]{2,1,0:T(8,128)(2,1)S(1)} all-gather(bf16[24,24,128]{2,1,0:T(8,128)(2,1)S(1)} %get-tuple-element.7), channel_id=1, replica_groups=mesh['crops'=2,'row'=4,'col'=4] {'col'}, dimensions={1}, use_global_device_ids=true | all-gather | bytes 737280 | tf_op jit(solution)/shard_map/all_gather | solution.py:70
  44.4 1.3 %copy.43 = bf16[24,96,128]{1,0,2:T(8,128)(2,1)} copy(bf16[24,96,128]{2,1,0:T(8,128)(2,1)S(1)} %all_gather.13) | data formatting | bytes 1179648 | tf_op jit(solution)/shard_map/all_gather | solution.py:70
  45.7 6.7 %all_gather.12 = bf16[24,96,128]{2,1,0:T(8,128)(2,1)S(1)} all-gather(bf16[24,24,128]{2,1,0:T(8,128)(2,1)S(1)} %broadcast_select_fusion.3), channel_id=1, replica_groups=mesh['crops'=2,'row'=4,'col'=4] {'row'}, dimensions={1}, use_global_device_ids=true | all-gather | bytes 737280 | tf_op jit(solution)/shard_map/all_gather | solution.py:66
  52.4 1.3 %copy.42 = bf16[24,96,128]{1,0,2:T(8,128)(2,1)} copy(bf16[24,96,128]{2,1,0:T(8,128)(2,1)S(1)} %all_gather.12) | data formatting | bytes 1179648 | tf_op jit(solution)/shard_map/all_gather | solution.py:66
  53.6 1.9 %bitcast_reduce_fusion.1 = (f32[24,24]{0,1:T(8,128)S(1)}, f32[128,24,24]{2,1,0:T(8,128)S(1)}) fusion(bf16[24,96,128]{1,0,2:T(8,128)(2,1)} %copy.42, bf16[24,96,128]{1,0,2:T(8,128)(2,1)} %copy.43), kind=kOutput, calls=%fused_computation.1 | convolution fusion | flops 14228928 | bytes 1476864 | tf_op jit(solution)/shard_map/ikc,jkc->ijc/dot_general | solution.py:68
  55.6 0.0 copy-start.1
  55.6 0.0 copy-start.5
  55.6 0.1 copy.46
  55.7 1.2 copy.44
  56.9 1.3 %multiply_reduce_fusion.2 = f32[24,24]{1,0:T(8,128)S(1)} fusion(f32[128,24,24]{0,1,2:T(8,128)} %copy.44, f32[24,24]{1,0:T(8,128)S(1)} %broadcast_multiply_fusion.2), kind=kLoop, calls=%fused_computation.49 | loop fusion | flops 220608 | bytes 299520 | tf_op jit(solution)/shard_map/reduce_sum | solution.py:15
  58.2 1.4 %fusion.59 = (f32[24,24]{1,0:T(8,128)S(1)}, f32[24,24,128]{2,1,0:T(8,128)S(1)}) fusion(bf16[2,128,128]{2,1,0:T(8,128)(2,1)S(1)} %copy-done.5, f32[128,24,24]{0,1,2:T(8,128)} %copy.44, f32[128]{0:T(128)S(1)} %get-tuple-element.12, f32[128]{0:T(128)S(1)} %get-tuple-element.13, f32[24,24]{1,0:T(8,128)S(1)} %add_rsqrt_fusion.2, ...), kind=kOutput, calls=%fused_computation.107 | convolution fusion | flops 19832256 | bytes 1244416 | tf_op jit(solution)/shard_map/ijc,cd->ijd/dot_general | solution.py:38
  59.6 0.0 copy-start.2
  59.6 0.3 multiply_reduce_fusion.1
  59.9 0.5 fusion.29
  60.5 1.1 copy-done
  61.6 0.2 fusion.2
  61.8 1.9 %collective-permute-start.4 = (bf16[24,24,128]{2,1,0:T(8,128)(2,1)S(1)}, bf16[24,24,128]{2,1,0:T(8,128)(2,1)S(1)}, u32[]{:S(2)}, u32[]{:S(2)}) collective-permute-start(bf16[24,24,128]{2,1,0:T(8,128)(2,1)S(1)} %get-tuple-element.5), channel_id=1, source_target_pairs={{0,1},{1,0},{2,3},{3,2},{4,5},{5,4},{6,7},{7,6},{8,9},{9,8},{10,11... | collective-permute-start | bytes 442376 | tf_op jit(solution)/shard_map/ppermute | solution.py:10
  63.6 4.4 %collective-permute-done.4 = bf16[24,24,128]{2,1,0:T(8,128)(2,1)S(1)} collective-permute-done((bf16[24,24,128]{2,1,0:T(8,128)(2,1)S(1)}, bf16[24,24,128]{2,1,0:T(8,128)(2,1)S(1)}, u32[]{:S(2)}, u32[]{:S(2)}) %collective-permute-start.4) | collective-permute-done | bytes 147488 | tf_op jit(solution)/shard_map/ppermute | solution.py:10
  68.0 1.4 %collective-permute-done.5 = bf16[24,24,128]{2,1,0:T(8,128)(2,1)S(1)} collective-permute-done((bf16[24,24,128]{2,1,0:T(8,128)(2,1)S(1)}, bf16[24,24,128]{2,1,0:T(8,128)(2,1)S(1)}, u32[]{:S(2)}, u32[]{:S(2)}) %collective-permute-start.5) | collective-permute-done | bytes 147488 | tf_op jit(solution)/shard_map/ppermute | solution.py:10
  69.4 2.6 %collective-permute-start.6 = (bf16[24,24,128]{2,1,0:T(8,128)(2,1)S(1)}, bf16[24,24,128]{2,1,0:T(8,128)(2,1)S(1)}, u32[]{:S(2)}, u32[]{:S(2)}) collective-permute-start(bf16[24,24,128]{2,1,0:T(8,128)(2,1)S(1)} %broadcast_select_fusion), channel_id=1, source_target_pairs={{0,2},{1,3},{2,0},{3,1},{4,6},{5,7},{6,4},{7,5},{8,10},{9,11},{10,... | collective-permute-start | bytes 442376 | tf_op jit(solution)/shard_map/ppermute | solution.py:10
  72.0 7.5 %collective-permute-done.6 = bf16[24,24,128]{2,1,0:T(8,128)(2,1)S(1)} collective-permute-done((bf16[24,24,128]{2,1,0:T(8,128)(2,1)S(1)}, bf16[24,24,128]{2,1,0:T(8,128)(2,1)S(1)}, u32[]{:S(2)}, u32[]{:S(2)}) %collective-permute-start.6) | collective-permute-done | bytes 147488 | tf_op jit(solution)/shard_map/ppermute | solution.py:10
  79.4 1.4 %collective-permute-start.7 = (bf16[24,24,128]{2,1,0:T(8,128)(2,1)S(1)}, bf16[24,24,128]{2,1,0:T(8,128)(2,1)S(1)}, u32[]{:S(2)}, u32[]{:S(2)}) collective-permute-start(bf16[24,24,128]{2,1,0:T(8,128)(2,1)S(1)} %collective-permute-done.6), channel_id=1, source_target_pairs={{0,8},{1,9},{2,10},{3,11},{4,12},{5,13},{6,14},{7,15},{8,0},{9,1},... | collective-permute-start | bytes 442376 | tf_op jit(solution)/shard_map/ppermute | solution.py:10
  80.8 7.8 %all_gather.14 = bf16[96,24,128]{2,1,0:T(8,128)(2,1)S(1)} all-gather(bf16[24,24,128]{2,1,0:T(8,128)(2,1)S(1)} %get-tuple-element.6), channel_id=1, replica_groups=mesh['crops'=2,'row'=4,'col'=4] {'row'}, dimensions={0}, use_global_device_ids=true | all-gather | bytes 737280 | tf_op jit(solution)/shard_map/all_gather | solution.py:82
  88.6 1.4 %copy.49 = bf16[96,24,128]{0,1,2:T(8,128)(2,1)} copy(bf16[96,24,128]{2,1,0:T(8,128)(2,1)S(1)} %all_gather.14) | data formatting | bytes 1179648 | tf_op jit(solution)/shard_map/all_gather | solution.py:82
  90.0 0.0 collective-permute-done.7
  90.1 17.9 %all_gather.15 = bf16[96,24,128]{2,1,0:T(8,128)(2,1)} all-gather(bf16[24,24,128]{2,1,0:T(8,128)(2,1)S(1)} %broadcast_select_fusion.2), channel_id=1, replica_groups=mesh['crops'=2,'row'=4,'col'=4] {'col'}, dimensions={0}, use_global_device_ids=true | all-gather | bytes 737280 | tf_op jit(solution)/shard_map/all_gather | solution.py:77
  108.0 5.2 %copy.50 = bf16[96,24,128]{1,0,2:T(8,128)(2,1)S(1)} copy(bf16[96,24,128]{2,1,0:T(8,128)(2,1)} %all_gather.15) | data formatting | bytes 1179648 | tf_op jit(solution)/shard_map/all_gather | solution.py:77
  113.3 3.2 %bitcast_reduce_fusion = (f32[24,24]{0,1:T(8,128)S(1)}, f32[128,24,24]{2,1,0:T(8,128)}) fusion(bf16[96,24,128]{0,1,2:T(8,128)(2,1)} %copy.49, bf16[96,24,128]{1,0,2:T(8,128)(2,1)S(1)} %copy.50), kind=kOutput, calls=%fused_computation | convolution fusion | flops 14228928 | bytes 1476864 | tf_op jit(solution)/shard_map/kic,kjc->ijc/dot_general | solution.py:79
  116.5 0.1 copy.53
  116.6 1.9 %copy.51 = f32[128,24,24]{0,1,2:T(8,128)S(1)} copy(f32[128,24,24]{2,1,0:T(8,128)} %get-tuple-element.26) | data formatting | bytes 589824 | tf_op jit(solution)/shard_map/kic,kjc->ijc/dot_general | solution.py:79
  118.5 0.3 multiply_reduce_fusion
  118.8 2.0 %fusion = f32[24,24,128]{2,1,0:T(8,128)} fusion(f32[24,24,128]{2,1,0:T(8,128)S(1)} %copy-done.3, f32[24,24,640]{2,1,0:T(8,128)} %copy-done, f32[128,24,24]{0,1,2:T(8,128)S(1)} %copy.51, f32[128]{0:T(128)S(1)} %get-tuple-element.16, f32[128]{0:T(128)S(1)} %get-tuple-element.9, f32[24,24]{1,0:T(8,128)S(1)} %add_rsqrt_fusion, ...), kind=kOutput, calls=%fused_computation.3 | convolution fusion | flops 19611648 | bytes 1238016 | tf_op jit(solution)/shard_map/ijc,cd->ijd/dot_general | solution.py:38
  (22 shorter events, 0.1 us)
Async XLA Ops:
  7.6 6.9 %collective-permute-start = (bf16[24,24,128]{2,1,0:T(8,128)(2,1)S(1)}, bf16[24,24,128]{2,1,0:T(8,128)(2,1)S(1)}, u32[]{:S(2)}, u32[]{:S(2)}) collective-permute-start(bf16[24,24,128]{2,1,0:T(8,128)(2,1)S(1)} %get-tuple-element.8), channel_id=1, source_target_pairs={{0,1},{1,0},{2,3},{3,2},{4,5},{5,4},{6,7},{7,6},{8,9},{9,8},{10,11... | collective-permute-start | bytes 442376 | tf_op jit(solution)/shard_map/ppermute | solution.py:10
  14.5 1.4 %collective-permute-start.1 = (bf16[24,24,128]{2,1,0:T(8,128)(2,1)S(1)}, bf16[24,24,128]{2,1,0:T(8,128)(2,1)S(1)}, u32[]{:S(2)}, u32[]{:S(2)}) collective-permute-start(bf16[24,24,128]{2,1,0:T(8,128)(2,1)S(1)} %collective-permute-done), channel_id=1, source_target_pairs={{0,4},{1,5},{2,6},{3,7},{4,0},{5,1},{6,2},{7,3},{8,12},{9,13},{10,... | collective-permute-start | bytes 442376 | tf_op jit(solution)/shard_map/ppermute | solution.py:10
  15.9 10.1 %collective-permute-start.2 = (bf16[24,24,128]{2,1,0:T(8,128)(2,1)S(1)}, bf16[24,24,128]{2,1,0:T(8,128)(2,1)S(1)}, u32[]{:S(2)}, u32[]{:S(2)}) collective-permute-start(bf16[24,24,128]{2,1,0:T(8,128)(2,1)S(1)} %broadcast_select_fusion.1), channel_id=1, source_target_pairs={{0,2},{1,3},{2,0},{3,1},{4,6},{5,7},{6,4},{7,5},{8,10},{9,11},{10,... | collective-permute-start | bytes 442376 | tf_op jit(solution)/shard_map/ppermute | solution.py:10
  26.1 19.6 %collective-permute-start.3 = (bf16[24,24,128]{2,1,0:T(8,128)(2,1)S(1)}, bf16[24,24,128]{2,1,0:T(8,128)(2,1)S(1)}, u32[]{:S(2)}, u32[]{:S(2)}) collective-permute-start(bf16[24,24,128]{2,1,0:T(8,128)(2,1)S(1)} %collective-permute-done.2), channel_id=1, source_target_pairs={{0,8},{1,9},{2,10},{3,11},{4,12},{5,13},{6,14},{7,15},{8,0},{9,1},... | collective-permute-start | bytes 442376 | tf_op jit(solution)/shard_map/ppermute | solution.py:10
  55.6 2.6 %copy-start.1 = (f32[24,24,128]{2,1,0:T(8,128)S(1)}, f32[24,24,128]{2,1,0:T(8,128)}, u32[]{:S(2)}) copy-start(f32[24,24,128]{2,1,0:T(8,128)} %param.7) | copy-start | bytes 884740
  55.6 2.6 %copy-start.5 = (bf16[2,128,128]{2,1,0:T(8,128)(2,1)S(1)}, bf16[2,128,128]{2,1,0:T(8,128)(2,1)}, u32[]{:S(2)}) copy-start(bf16[2,128,128]{2,1,0:T(8,128)(2,1)} %param.13) | copy-start | bytes 196612
  56.9 3.1 %copy-start.4 = (bf16[2,128,640]{2,1,0:T(8,128)(2,1)S(1)}, bf16[2,128,640]{2,1,0:T(8,128)(2,1)}, u32[]{:S(2)}) copy-start(bf16[2,128,640]{2,1,0:T(8,128)(2,1)} %param.12) | copy-start | bytes 983044
  59.6 2.2 %copy-start.2 = (f32[24,24,128]{2,1,0:T(8,128)}, f32[24,24,128]{2,1,0:T(8,128)S(1)}, u32[]{:S(2)}) copy-start(f32[24,24,128]{2,1,0:T(8,128)S(1)} %get-tuple-element.24) | copy-start | bytes 884740
  60.5 1.1 copy-start
  61.8 6.2 %collective-permute-start.4 = (bf16[24,24,128]{2,1,0:T(8,128)(2,1)S(1)}, bf16[24,24,128]{2,1,0:T(8,128)(2,1)S(1)}, u32[]{:S(2)}, u32[]{:S(2)}) collective-permute-start(bf16[24,24,128]{2,1,0:T(8,128)(2,1)S(1)} %get-tuple-element.5), channel_id=1, source_target_pairs={{0,1},{1,0},{2,3},{3,2},{4,5},{5,4},{6,7},{7,6},{8,9},{9,8},{10,11... | collective-permute-start | bytes 442376 | tf_op jit(solution)/shard_map/ppermute | solution.py:10
  68.0 1.4 %collective-permute-start.5 = (bf16[24,24,128]{2,1,0:T(8,128)(2,1)S(1)}, bf16[24,24,128]{2,1,0:T(8,128)(2,1)S(1)}, u32[]{:S(2)}, u32[]{:S(2)}) collective-permute-start(bf16[24,24,128]{2,1,0:T(8,128)(2,1)S(1)} %collective-permute-done.4), channel_id=1, source_target_pairs={{0,4},{1,5},{2,6},{3,7},{4,0},{5,1},{6,2},{7,3},{8,12},{9,13},{10,... | collective-permute-start | bytes 442376 | tf_op jit(solution)/shard_map/ppermute | solution.py:10
  69.4 10.0 %collective-permute-start.6 = (bf16[24,24,128]{2,1,0:T(8,128)(2,1)S(1)}, bf16[24,24,128]{2,1,0:T(8,128)(2,1)S(1)}, u32[]{:S(2)}, u32[]{:S(2)}) collective-permute-start(bf16[24,24,128]{2,1,0:T(8,128)(2,1)S(1)} %broadcast_select_fusion), channel_id=1, source_target_pairs={{0,2},{1,3},{2,0},{3,1},{4,6},{5,7},{6,4},{7,5},{8,10},{9,11},{10,... | collective-permute-start | bytes 442376 | tf_op jit(solution)/shard_map/ppermute | solution.py:10
  79.4 10.6 %collective-permute-start.7 = (bf16[24,24,128]{2,1,0:T(8,128)(2,1)S(1)}, bf16[24,24,128]{2,1,0:T(8,128)(2,1)S(1)}, u32[]{:S(2)}, u32[]{:S(2)}) collective-permute-start(bf16[24,24,128]{2,1,0:T(8,128)(2,1)S(1)} %collective-permute-done.6), channel_id=1, source_target_pairs={{0,8},{1,9},{2,10},{3,11},{4,12},{5,13},{6,14},{7,15},{8,0},{9,1},... | collective-permute-start | bytes 442376 | tf_op jit(solution)/shard_map/ppermute | solution.py:10
  116.5 2.3 %copy-start.3 = (f32[24,24,128]{2,1,0:T(8,128)S(1)}, f32[24,24,128]{2,1,0:T(8,128)}, u32[]{:S(2)}) copy-start(f32[24,24,128]{2,1,0:T(8,128)} %copy-done.2) | copy-start | bytes 884740
where the time goes:
time: 121 us
  blocking collectives  49.2 us (41%)
  waiting for transfers between devices  25.7 us (21%)
  local copies, waits for them, and re-layouts  16 us (13%)
  starting transfers between devices  13.3 us (11%)
  matrix products  10.8 us (9%)
  other arithmetic  5.61 us (5%)
    ppermute x8, waiting for transfers between devices, partner_2(): return lax.ppermute(value, axis, pairs)  25.7 us
    all_gather x1, blocking collectives, body(): left_cols = lax.all_gather(partner, 'col', axis=0, tiled=True)  17.9 us
    all_gather x1, blocking collectives, body(): lax.all_gather(left, 'col', axis=1, tiled=True)  16.8 us
    ppermute x8, starting transfers between devices, partner_2(): return lax.ppermute(value, axis, pairs)  13.3 us
    all_gather x1, blocking collectives, body(): lax.all_gather(right, 'row', axis=0, tiled=True)  7.8 us
    all_gather x1, blocking collectives, body(): right_rows = lax.all_gather(partner, 'row', axis=1, tiled=True)  6.69 us
    all_gather x1, local copies, waits for them, and re-layouts, body(): left_cols = lax.all_gather(partner, 'col', axis=0, tiled=True)  5.24 us
    dot_general x2, matrix products, finish(): jnp.einsum('ijc,cd->ijd', tnorm, weight_out, preferred_element_type=jnp.f...  3.48 us
  transfers between devices with their start and end apart: 8, of which 6 were waited for; matrix products, arithmetic and copies ran while one was open for 2% of the time, Pallas kernels for 0%

commit v1 on v0

v1 whole, which is shorter than its diff:
```python
import functools

import jax
import jax.numpy as jnp
from jax import lax
from jax.experimental import pallas as pl
from jax.experimental.pallas import tpu as pltpu
from jax.sharding import PartitionSpec as P

F32 = jnp.float32
BF16 = jnp.bfloat16
MESH = pl.DeviceIdType.MESH
CHUNKS = 6


def xor(a, b, n):
    total = 0
    bit = 1
    while bit < n:
        x, y = (a // bit) % 2, (b // bit) % 2
        total = total + bit * (x + y - 2 * x * y)
        bit *= 2
    return total


def layer_norm(value, gain, bias):
    mean = jnp.mean(value, axis=-1, keepdims=True)
    centered = value - mean
    spread = jnp.mean(centered * centered, axis=-1, keepdims=True)
    return centered * lax.rsqrt(spread + 1e-05) * gain + bias


def products(left, right, out, size, stride_i, stride_k, group=8):
    def step(index, carry):
        first = index * group
        sums = [jnp.zeros((size, left.shape[-1]), F32) for _ in range(group)]
        for k in range(size):
            right_k = right[k * size : (k + 1) * size, :]
            for i in range(group):
                one = left[pl.ds((first + i) * stride_i + k * stride_k, 1), :]
                sums[i] = sums[i] + one * right_k
        for i in range(group):
            out[pl.ds(pl.multiple_of((first + i) * size, 8), size), :] = sums[i]
        return carry

    lax.fori_loop(0, size // group, step, 0)


def kernel(
    n,
    size,
    pair,
    mask,
    chain,
    table,
    norms,
    w_in,
    w_out,
    out,
    state,
    gating,
    masking,
    own_left,
    own_right,
    operand,
    triangle,
    total,
    right_slots,
    left_slots,
    part_one,
    part_two,
    got_one,
    got_two,
    send_right,
    recv_right,
    send_left,
    recv_left,
    send_one,
    recv_one,
    send_two,
    recv_two,
):
    row, col = lax.axis_index("row"), lax.axis_index("col")
    crop = lax.axis_index("crops")
    width = pair.shape[-1]
    rows = size * size
    piece = rows // CHUNKS

    barrier = pltpu.get_barrier_semaphore()
    for s in range(1, n):
        pl.semaphore_signal(
            barrier, inc=1, device_id=(crop, xor(row, s, n), col), device_id_type=MESH
        )
        pl.semaphore_signal(
            barrier, inc=1, device_id=(crop, row, xor(col, s, n)), device_id_type=MESH
        )

    sub = lax.broadcasted_iota(jnp.int32, (size, width), 0)
    columns = jnp.zeros((size, width), jnp.int32)
    for j in range(size):
        columns = jnp.where(sub == j, chain[col * size + j], columns)
    turned = mask[...].astype(F32).T
    for i in range(size):
        same = columns == chain[row * size + i]
        at = slice(i * size, (i + 1) * size)
        state[at, :] = pair[i] + jnp.where(same, table[1:2, :], table[0:1, :])
        masking[at, :] = jnp.broadcast_to(turned[:, i : i + 1], (size, width))

    def inputs_of(u, left_to, right_to):
        for part in range(CHUNKS):
            at = slice(part * piece, (part + 1) * piece)
            normed = layer_norm(state[at, :], norms[u, 0:1, :], norms[u, 1:2, :]).astype(BF16)
            projected = jnp.dot(normed, w_in[u], preferred_element_type=F32)
            block = [projected[:, b * width : (b + 1) * width] for b in range(5)]
            here = masking[at, :]
            left_to(part, at, here * jax.nn.sigmoid(block[1]) * block[0])
            right_to(part, at, here * jax.nn.sigmoid(block[3]) * block[2])
            gating[at, :] = jax.nn.sigmoid(block[4])

    def finish(u, put):
        for part in range(CHUNKS):
            at = slice(part * piece, (part + 1) * piece)
            tnorm = layer_norm(total[at, :], norms[u, 2:3, :], norms[u, 3:4, :]).astype(BF16)
            put(
                part,
                at,
                state[at, :]
                + gating[at, :] * jnp.dot(tnorm, w_out[u], preferred_element_type=F32),
            )

    def put_f32(ref):
        def put(part, at, value):
            ref[at, :] = value

        return put

    def put_rounded(ref):
        def put(part, at, value):
            ref[at, :] = value.astype(BF16).astype(F32)

        return put

    def copy(src, dst, send, recv, to):
        return pltpu.make_async_remote_copy(
            src_ref=src,
            dst_ref=dst,
            send_sem=send,
            recv_sem=recv,
            device_id=to,
            device_id_type=MESH,
        )

    def right_copy(s):
        return copy(
            right_slots.at[0],
            right_slots.at[s],
            send_right.at[s],
            recv_right.at[s],
            (crop, xor(row, s, n), col),
        )

    def left_copy(s):
        return copy(
            left_slots.at[0],
            left_slots.at[s],
            send_left.at[s],
            recv_left.at[s],
            (crop, row, xor(col, s, n)),
        )

    def one_copy(s):
        return copy(
            part_one.at[s], got_one.at[s], send_one.at[s], recv_one.at[s],
            (crop, row, xor(col, s, n)),
        )

    def two_copy(s):
        return copy(
            part_two.at[s], got_two.at[s], send_two.at[s], recv_two.at[s],
            (crop, xor(row, s, n), col),
        )

    inputs_of(0, put_rounded(own_left), put_f32(own_right))
    pairs = 2 * size
    for k in range(0, size, 2):
        both = [own_right[pl.ds(k + d, size, stride=size), :] for d in range(2)]
        right_slots[0, k * size : k * size + pairs, :] = jnp.concatenate(both, axis=0).astype(BF16)
    pl.semaphore_wait(barrier, 2 * (n - 1))
    for s in range(1, n):
        right_copy(s).start()

    def outgoing(s, carry):
        @pl.when(s > 0)
        def _():
            right_copy(s).wait_recv()

        operand[...] = right_slots[s].astype(F32)
        products(own_left, operand, triangle, size, size, 1)
        slot = xor(col, xor(row, s, n), n)

        @pl.when(slot == 0)
        def _():
            total[...] = triangle[...]

        @pl.when(slot > 0)
        def _():
            part_one[slot] = triangle[...].astype(BF16)
            one_copy(slot).start()

        return carry

    lax.fori_loop(0, n, outgoing, 0)
    for s in range(1, n):
        one_copy(s).wait_recv()
        total[...] += got_one[s].astype(F32)
    finish(0, put_f32(state))

    def left_to(part, at, value):
        left_slots[0, at, :] = value.astype(BF16)

    inputs_of(1, left_to, put_rounded(own_right))
    for s in range(1, n):
        left_copy(s).start()

    def incoming(s, carry):
        @pl.when(s > 0)
        def _():
            left_copy(s).wait_recv()

        operand[...] = left_slots[s].astype(F32)
        products(operand, own_right, triangle, size, 1, size)
        slot = xor(row, xor(col, s, n), n)

        @pl.when(slot == 0)
        def _():
            total[...] = triangle[...]

        @pl.when(slot > 0)
        def _():
            part_two[slot] = triangle[...].astype(BF16)
            two_copy(slot).start()

        return carry

    lax.fori_loop(0, n, incoming, 0)
    for s in range(1, n):
        two_copy(s).wait_recv()
        total[...] += got_two[s].astype(F32)

    def put_out(part, at, value):
        lines = piece // size
        out[part * lines : (part + 1) * lines] = value.reshape(lines, size, width)

    finish(1, put_out)
    for s in range(1, n):
        right_copy(s).wait_send()
        one_copy(s).wait_send()
        left_copy(s).wait_send()
        two_copy(s).wait_send()


def body(pair, pair_mask, chain_ids, chain_pair_table, norms, w_in, w_out):
    n = lax.axis_size("row")
    size, _, width = pair.shape
    rows = size * size
    vmem = pl.BlockSpec(memory_space=pltpu.VMEM)
    smem = pl.BlockSpec(memory_space=pltpu.SMEM)
    flat = pltpu.VMEM((rows, width), F32)
    slots = pltpu.VMEM((n, rows, width), BF16)
    return pl.pallas_call(
        functools.partial(kernel, n, size),
        out_shape=jax.ShapeDtypeStruct(pair.shape, F32),
        in_specs=[vmem, vmem, smem, vmem, vmem, vmem, vmem],
        out_specs=vmem,
        scratch_shapes=[flat] * 8 + [slots] * 6 + [pltpu.SemaphoreType.DMA((n,))] * 8,
        compiler_params=pltpu.CompilerParams(
            collective_id=0, has_side_effects=True, vmem_limit_bytes=40 * 1024 * 1024
        ),
    )(pair, pair_mask, chain_ids, chain_pair_table, norms, w_in, w_out)


def solution(mesh):
    placed = (
        P(("crops", "row"), "col", None),
        P(("crops", "row"), "col"),
        P("crops"),
        P(),
        P(),
        P(),
        P(),
    )
    return jax.shard_map(
        body,
        mesh=mesh,
        in_specs=placed,
        out_specs=P(("crops", "row"), "col", None),
        check_vma=False,
    )
```

time: 121 us -> 52.2 us (0.43)
  blocking collectives: 49.2 us -> 0 us
  Pallas kernels: 0 us -> 45 us
  waiting for transfers between devices: 25.7 us -> 0 us
  starting transfers between devices: 13.3 us -> 0 us
  matrix products: 10.8 us -> 0 us
  local copies, waits for them, and re-layouts: 16 us -> 6.21 us
  other arithmetic: 5.61 us -> 0 us
    all_gather x4 -> x0, blocking collectives: 49.2 us -> none  [the longest x1 17.9 us: body(): left_cols = lax.all_gather(partner, 'col', axis=0, tiled=True)]
    pallas_call x0 -> x1, Pallas kernels: none -> 45 us  [body(): pl.pallas_call(functools.partial(kernel, n, size), out_shape=jax.ShapeDty...]
    ppermute x8 -> x0, waiting for transfers between devices: 25.7 us -> none  [partner_2(): return lax.ppermute(value, axis, pairs)]
    ppermute x8 -> x0, starting transfers between devices: 13.3 us -> none  [partner_2(): return lax.ppermute(value, axis, pairs)]
    dot_general x6 -> x0, matrix products: 10.8 us -> none  [the longest x2 3.48 us: finish(): jnp.einsum('ijc,cd->ijd', tnorm, weight_out, preferred_element_type=jnp.f...]
    all_gather x4 -> x0, local copies, waits for them, and re-layouts: 9.22 us -> none  [the longest x1 5.24 us: body(): left_cols = lax.all_gather(partner, 'col', axis=0, tiled=True)]
    unnamed x12 -> x15, local copies, waits for them, and re-layouts: 1.13 us -> 6.21 us
    reduce_sum x5 -> x0, other arithmetic: 4.32 us -> none  [the longest x4 3.09 us: layer_norm(): spread = jnp.mean(jnp.square(value - mean), axis=-1, keepdims=True)]
  transfers between devices with their start and end apart: 8 -> 0, of which waited for: 6 -> 0; matrix products, arithmetic and copies ran while one was open for 2% -> 0% of each run, Pallas kernels for 0% -> 0%
where the time goes in v1:
time: 52.2 us; the launch traced here: 51.2 us
  Pallas kernels  45 us (86%)
  local copies, waits for them, and re-layouts  6.21 us (12%)
    pallas_call x1, Pallas kernels, body(): pl.pallas_call(functools.partial(kernel, n, size), out_shape=jax.ShapeDty...  45 us
    unnamed x15, local copies, waits for them, and re-layouts  6.21 us

profile of v1, /device:TPU:0, one launch (start us, length us, event | category | flops | bytes accessed | tf_op | source)
XLA Modules:
  0.0 51.2 jit_solution(2759090934475914695)
XLA Ops:
  0.0 0.0 copy-start
  0.0 1.0 %copy-done = bf16[2,128,640]{2,1,0:T(8,128)(2,1)S(1)} copy-done((bf16[2,128,640]{2,1,0:T(8,128)(2,1)S(1)}, bf16[2,128,640]{2,1,0:T(8,128)(2,1)}, u32[]{:S(2)}) %copy-start) | copy-done | bytes 327704
  1.0 0.0 copy-start.1
  1.0 1.0 %copy-done.1 = f32[24,24,128]{2,1,0:T(8,128)S(1)} copy-done((f32[24,24,128]{2,1,0:T(8,128)S(1)}, f32[24,24,128]{2,1,0:T(8,128)}, u32[]{:S(2)}) %copy-start.1) | copy-done | bytes 294936
  1.9 0.0 copy-start.2
  1.9 0.8 %copy-done.2 = bf16[2,128,128]{2,1,0:T(8,128)(2,1)S(1)} copy-done((bf16[2,128,128]{2,1,0:T(8,128)(2,1)S(1)}, bf16[2,128,128]{2,1,0:T(8,128)(2,1)}, u32[]{:S(2)}) %copy-start.2) | copy-done | bytes 65560
  2.8 0.0 copy-start.3
  2.8 0.7 %copy-done.3 = s32[24,24]{1,0:T(8,128)S(1)} copy-done((s32[24,24]{1,0:T(8,128)S(1)}, s32[24,24]{1,0:T(8,128)}, u32[]{:S(2)}) %copy-start.3) | copy-done | bytes 2328
  3.5 0.0 copy-start.4
  3.5 0.7 %copy-done.4 = f32[2,4,128]{2,1,0:T(4,128)S(1)} copy-done((f32[2,4,128]{2,1,0:T(4,128)S(1)}, f32[2,4,128]{2,1,0:T(4,128)}, u32[]{:S(2)}) %copy-start.4) | copy-done | bytes 4120
  4.2 0.0 copy-start.5
  4.2 0.7 %copy-done.5 = f32[2,128]{1,0:T(2,128)S(1)} copy-done((f32[2,128]{1,0:T(2,128)S(1)}, f32[2,128]{1,0:T(2,128)}, u32[]{:S(2)}) %copy-start.5) | copy-done | bytes 1048
  4.8 0.0 copy-start.6
  4.9 0.7 %copy-done.6 = s32[96]{0:T(128)S(1)} copy-done((s32[96]{0:T(128)S(1)}, s32[96]{0:T(128)}, u32[]{:S(2)}) %copy-start.6) | copy-done | bytes 408
  5.5 45.0 %shard_map.73 = f32[24,24,128]{2,1,0:T(8,128)S(1)} custom-call(f32[24,24,128]{2,1,0:T(8,128)S(1)} %copy-done.1, s32[24,24]{1,0:T(8,128)S(1)} %copy-done.3, s32[96]{0:T(128)S(1)} %copy-done.6, f32[2,128]{1,0:T(2,128)S(1)} %copy-done.5, f32[2,4,128]{2,1,0:T(4,128)S(1)} %copy-done.4, bf16[2,128,640]{2,1,0:T(8,128)(2,1)S(1)} %copy-done, ...), custom_call_target="tpu_custom_call" | custom-call | tf_op jit(solution)/shard_map/pallas_call | solution.py:270
  50.5 0.7 %copy.9 = f32[24,24,128]{2,1,0:T(8,128)} copy(f32[24,24,128]{2,1,0:T(8,128)S(1)} %shard_map.73) | data formatting | bytes 589824
Async XLA Ops:
  0.0 1.0 %copy-start = (bf16[2,128,640]{2,1,0:T(8,128)(2,1)S(1)}, bf16[2,128,640]{2,1,0:T(8,128)(2,1)}, u32[]{:S(2)}) copy-start(bf16[2,128,640]{2,1,0:T(8,128)(2,1)} %w_in.1) | copy-start | bytes 983044
  1.0 1.0 %copy-start.1 = (f32[24,24,128]{2,1,0:T(8,128)S(1)}, f32[24,24,128]{2,1,0:T(8,128)}, u32[]{:S(2)}) copy-start(f32[24,24,128]{2,1,0:T(8,128)} %pair.1) | copy-start | bytes 884740
  1.9 0.8 %copy-start.2 = (bf16[2,128,128]{2,1,0:T(8,128)(2,1)S(1)}, bf16[2,128,128]{2,1,0:T(8,128)(2,1)}, u32[]{:S(2)}) copy-start(bf16[2,128,128]{2,1,0:T(8,128)(2,1)} %w_out.1) | copy-start | bytes 196612
  2.8 0.7 %copy-start.3 = (s32[24,24]{1,0:T(8,128)S(1)}, s32[24,24]{1,0:T(8,128)}, u32[]{:S(2)}) copy-start(s32[24,24]{1,0:T(8,128)} %mask.1) | copy-start | bytes 6916
  3.5 0.7 %copy-start.4 = (f32[2,4,128]{2,1,0:T(4,128)S(1)}, f32[2,4,128]{2,1,0:T(4,128)}, u32[]{:S(2)}) copy-start(f32[2,4,128]{2,1,0:T(4,128)} %norms.1) | copy-start | bytes 12292
  4.2 0.7 %copy-start.5 = (f32[2,128]{1,0:T(2,128)S(1)}, f32[2,128]{1,0:T(2,128)}, u32[]{:S(2)}) copy-start(f32[2,128]{1,0:T(2,128)} %table.1) | copy-start | bytes 3076
  4.8 0.7 %copy-start.6 = (s32[96]{0:T(128)S(1)}, s32[96]{0:T(128)}, u32[]{:S(2)}) copy-start(s32[96]{0:T(128)} %chain.1) | copy-start | bytes 1156

commit v2 on v0

v2 whole, which is shorter than its diff:
```python
import functools

import jax
import jax.numpy as jnp
from jax import lax
from jax.experimental import pallas as pl
from jax.experimental.pallas import tpu as pltpu
from jax.sharding import PartitionSpec as P

F32 = jnp.float32
BF16 = jnp.bfloat16
MESH = pl.DeviceIdType.MESH
LINES = 8


def xor(a, b, n):
    total = 0
    bit = 1
    while bit < n:
        x, y = (a // bit) % 2, (b // bit) % 2
        total = total + bit * (x + y - 2 * x * y)
        bit *= 2
    return total


def layer_norm(value, gain, bias):
    mean = jnp.mean(value, axis=-1, keepdims=True)
    centered = value - mean
    spread = jnp.mean(centered * centered, axis=-1, keepdims=True)
    return centered * lax.rsqrt(spread + 1e-05) * gain + bias


def kernel(
    n,
    size,
    pair_hbm,
    mask_hbm,
    chain_hbm,
    table_hbm,
    norms_hbm,
    w_in_hbm,
    w_out_hbm,
    out,
    pair,
    mask,
    chain,
    table,
    norms,
    w_in,
    w_out,
    normed,
    state,
    gating,
    masking,
    own_left,
    own_right,
    operand,
    triangle,
    total,
    right_slots,
    left_slots,
    part_one,
    part_two,
    got_one,
    got_two,
    load,
    send_right,
    recv_right,
    send_left,
    recv_left,
    send_one,
    recv_one,
    send_two,
    recv_two,
):
    row, col = lax.axis_index("row"), lax.axis_index("col")
    crop = lax.axis_index("crops")
    width = pair.shape[-1]
    count = size // LINES
    piece = size * LINES
    part = LINES * LINES

    loads = [
        pltpu.make_async_copy(source, target, load.at[index])
        for index, (source, target) in enumerate(
            (
                (pair_hbm, pair),
                (mask_hbm, mask),
                (chain_hbm, chain),
                (table_hbm, table),
                (norms_hbm, norms),
                (w_in_hbm, w_in),
                (w_out_hbm, w_out),
            )
        )
    ]
    for one in loads:
        one.start()

    barrier = pltpu.get_barrier_semaphore()
    for s in range(1, n):
        pl.semaphore_signal(
            barrier, inc=1, device_id=(crop, xor(row, s, n), col), device_id_type=MESH
        )
        pl.semaphore_signal(
            barrier, inc=1, device_id=(crop, row, xor(col, s, n)), device_id_type=MESH
        )

    def at(q):
        return slice(q * piece, (q + 1) * piece)

    def copy(slots_from, s_from, slots_to, s, q, send, recv, to):
        return pltpu.make_async_remote_copy(
            src_ref=slots_from.at[s_from, pl.ds(q * piece, piece), :],
            dst_ref=slots_to.at[s, pl.ds(q * piece, piece), :],
            send_sem=send.at[q, s],
            recv_sem=recv.at[q, s],
            device_id=to,
            device_id_type=MESH,
        )

    def along_row(s):
        return (crop, xor(row, s, n), col)

    def along_col(s):
        return (crop, row, xor(col, s, n))

    def right_copy(q, s):
        return copy(right_slots, 0, right_slots, s, q, send_right, recv_right, along_row(s))

    def left_copy(q, s):
        return copy(left_slots, 0, left_slots, s, q, send_left, recv_left, along_col(s))

    def one_copy(q, s):
        return copy(part_one, s, got_one, s, q, send_one, recv_one, along_col(s))

    def two_copy(q, s):
        return copy(part_two, s, got_two, s, q, send_two, recv_two, along_row(s))

    for index in (2, 1, 3, 0):
        loads[index].wait()
    sub = lax.broadcasted_iota(jnp.int32, (size, width), 0)
    columns = jnp.zeros((size, width), jnp.int32)
    for j in range(size):
        columns = jnp.where(sub == j, chain[col * size + j], columns)
    turned = mask[...].astype(F32).T
    for i in range(size):
        same = columns == chain[row * size + i]
        begin = pair[i] + jnp.where(same, table[1:2, :], table[0:1, :])
        held = jnp.broadcast_to(turned[:, i : i + 1], (size, width))
        for q in range(count):
            here = slice(q * piece + i * LINES, q * piece + (i + 1) * LINES)
            state[here, :] = begin[q * LINES : (q + 1) * LINES]
            masking[here, :] = held[q * LINES : (q + 1) * LINES]
    loads[4].wait()
    loads[5].wait()

    def norm(u, q):
        for half in range(2):
            h = slice(q * piece + half * (piece // 2), q * piece + (half + 1) * (piece // 2))
            normed[h, :] = layer_norm(state[h, :], norms[u, 0:1, :], norms[u, 1:2, :]).astype(BF16)

    def value_of(u, q, first):
        both = jnp.dot(
            normed[at(q), :],
            w_in[u, :, first * width : (first + 2) * width],
            preferred_element_type=F32,
        )
        return masking[at(q), :] * jax.nn.sigmoid(both[:, width:]) * both[:, :width]

    def gate_of(u, q):
        gating[at(q), :] = jax.nn.sigmoid(
            jnp.dot(normed[at(q), :], w_in[u, :, 4 * width :], preferred_element_type=F32)
        )

    def updated(u, where):
        tnorm = layer_norm(total[where, :], norms[u, 2:3, :], norms[u, 3:4, :]).astype(BF16)
        moved = jnp.dot(tnorm, w_out[u], preferred_element_type=F32)
        return state[where, :] + gating[where, :] * moved

    for q in range(count):
        norm(0, q)
        own_right[at(q), :] = value_of(0, q, 2)
    for q in range(count):
        for k in range(0, size, 2):
            both = [
                own_right[
                    pl.ds((k + d) // LINES * piece + q * part + (k + d) % LINES, LINES, stride=LINES), :
                ]
                for d in range(2)
            ]
            right_slots[0, q * piece + k * LINES : q * piece + (k + 2) * LINES, :] = (
                jnp.concatenate(both, axis=0).astype(BF16)
            )
        if q == 0:
            pl.semaphore_wait(barrier, 2 * (n - 1))
        for s in range(1, n):
            right_copy(q, s).start()
    for q in range(count):
        own_left[at(q), :] = value_of(0, q, 0).astype(BF16).astype(F32)
        gate_of(0, q)
    loads[6].wait()

    def outgoing(q):
        def step(s, carry):
            @pl.when(s > 0)
            def _():
                right_copy(q, s).wait_recv()

            operand[...] = right_slots[s, at(q), :].astype(F32)
            sums = [jnp.zeros((LINES, width), F32) for _ in range(size)]
            for k in range(size):
                right_k = operand[k * LINES : (k + 1) * LINES, :]
                for i in range(size):
                    line = k // LINES * piece + i * LINES + k % LINES
                    sums[i] = sums[i] + own_left[line : line + 1, :] * right_k
            for i in range(size):
                triangle[i * LINES : (i + 1) * LINES, :] = sums[i]
            slot = xor(col, xor(row, s, n), n)

            @pl.when(slot == 0)
            def _():
                total[at(q), :] = triangle[...]

            @pl.when(slot > 0)
            def _():
                part_one[slot, at(q), :] = triangle[...].astype(BF16)
                one_copy(q, slot).start()

            return carry

        lax.fori_loop(0, n, step, 0)

    def between(q):
        for s in range(1, n):
            one_copy(q, s).wait_recv()
        whole = total[at(q), :]
        for s in range(1, n):
            whole = whole + got_one[s, at(q), :].astype(F32)
        total[at(q), :] = whole
        state[at(q), :] = updated(0, at(q))
        norm(1, q)
        left_slots[0, at(q), :] = value_of(1, q, 0).astype(BF16)
        for s in range(1, n):
            left_copy(q, s).start()
        own_right[at(q), :] = value_of(1, q, 2).astype(BF16).astype(F32)
        gate_of(1, q)

    for q in range(count):
        outgoing(q)
        if q > 0:
            between(q - 1)
    between(count - 1)

    def incoming(q):
        def step(s, carry):
            @pl.when(s > 0)
            def _():
                left_copy(q, s).wait_recv()

            operand[...] = left_slots[s, at(q), :].astype(F32)
            sums = [[jnp.zeros((LINES, width), F32) for _ in range(LINES)] for _ in range(count)]
            for k in range(size):
                for b in range(count):
                    right_k = own_right[b * piece + k * LINES : b * piece + (k + 1) * LINES, :]
                    for i in range(LINES):
                        line = k * LINES + i
                        sums[b][i] = sums[b][i] + operand[line : line + 1, :] * right_k
            for b in range(count):
                for i in range(LINES):
                    to = b * part + i * LINES
                    triangle[to : to + LINES, :] = sums[b][i]
            slot = xor(row, xor(col, s, n), n)

            @pl.when(slot == 0)
            def _():
                for b in range(count):
                    to = b * piece + q * part
                    total[to : to + part, :] = triangle[b * part : (b + 1) * part, :]

            @pl.when(slot > 0)
            def _():
                part_two[slot, at(q), :] = triangle[...].astype(BF16)
                two_copy(q, slot).start()

            return carry

        lax.fori_loop(0, n, step, 0)

    def last(q):
        for s in range(1, n):
            two_copy(q, s).wait_recv()
        for b in range(count):
            to = slice(b * piece + q * part, b * piece + (q + 1) * part)
            whole = total[to, :]
            for s in range(1, n):
                begin = q * piece + b * part
                whole = whole + got_two[s, begin : begin + part, :].astype(F32)
            total[to, :] = whole
            out[q * LINES : (q + 1) * LINES, b * LINES : (b + 1) * LINES, :] = updated(
                1, to
            ).reshape(LINES, LINES, width)

    for q in range(count):
        incoming(q)
        if q > 0:
            last(q - 1)
    last(count - 1)
    for q in range(count):
        for s in range(1, n):
            right_copy(q, s).wait_send()
            one_copy(q, s).wait_send()
            left_copy(q, s).wait_send()
            two_copy(q, s).wait_send()


def body(pair, pair_mask, chain_ids, chain_pair_table, norms, w_in, w_out):
    n = lax.axis_size("row")
    size, _, width = pair.shape
    rows = size * size
    anywhere = pl.BlockSpec(memory_space=pl.ANY)
    flat = pltpu.VMEM((rows, width), F32)
    few = pltpu.VMEM((size * LINES, width), F32)
    slots = pltpu.VMEM((n, rows, width), BF16)
    inputs = (pair, pair_mask, chain_ids, chain_pair_table, norms, w_in, w_out)
    held = [
        (pltpu.SMEM if each is chain_ids else pltpu.VMEM)(each.shape, each.dtype)
        for each in inputs
    ]
    return pl.pallas_call(
        functools.partial(kernel, n, size),
        out_shape=jax.ShapeDtypeStruct(pair.shape, F32),
        in_specs=[anywhere] * len(inputs),
        out_specs=pl.BlockSpec(memory_space=pltpu.VMEM),
        scratch_shapes=held
        + [pltpu.VMEM((rows, width), BF16)]
        + [flat] * 5
        + [few] * 2
        + [flat]
        + [slots] * 6
        + [pltpu.SemaphoreType.DMA((len(inputs),))]
        + [pltpu.SemaphoreType.DMA((size // LINES, n))] * 8,
        compiler_params=pltpu.CompilerParams(
            collective_id=0, has_side_effects=True, vmem_limit_bytes=60 * 1024 * 1024
        ),
    )(*inputs)


def solution(mesh):
    placed = (
        P(("crops", "row"), "col", None),
        P(("crops", "row"), "col"),
        P("crops"),
        P(),
        P(),
        P(),
        P(),
    )
    return jax.shard_map(
        body,
        mesh=mesh,
        in_specs=placed,
        out_specs=P(("crops", "row"), "col", None),
        check_vma=False,
    )
```

time: 121 us -> 42.2 us (0.35)
  blocking collectives: 49.2 us -> 0 us
  Pallas kernels: 0 us -> 40.2 us
  waiting for transfers between devices: 25.7 us -> 0 us
  local copies, waits for them, and re-layouts: 16 us -> 1.69 us
  starting transfers between devices: 13.3 us -> 0 us
  matrix products: 10.8 us -> 0 us
  other arithmetic: 5.61 us -> 0 us
    all_gather x4 -> x0, blocking collectives: 49.2 us -> none  [the longest x1 17.9 us: body(): left_cols = lax.all_gather(partner, 'col', axis=0, tiled=True)]
    pallas_call x0 -> x1, Pallas kernels: none -> 40.2 us  [body(): pl.pallas_call(functools.partial(kernel, n, size), out_shape=jax.ShapeDty...]
    ppermute x8 -> x0, waiting for transfers between devices: 25.7 us -> none  [partner_2(): return lax.ppermute(value, axis, pairs)]
    ppermute x8 -> x0, starting transfers between devices: 13.3 us -> none  [partner_2(): return lax.ppermute(value, axis, pairs)]
    dot_general x6 -> x0, matrix products: 10.8 us -> none  [the longest x2 3.48 us: finish(): jnp.einsum('ijc,cd->ijd', tnorm, weight_out, preferred_element_type=jnp.f...]
    all_gather x4 -> x0, local copies, waits for them, and re-layouts: 9.22 us -> none  [the longest x1 5.24 us: body(): left_cols = lax.all_gather(partner, 'col', axis=0, tiled=True)]
    reduce_sum x5 -> x0, other arithmetic: 4.32 us -> none  [the longest x4 3.09 us: layer_norm(): spread = jnp.mean(jnp.square(value - mean), axis=-1, keepdims=True)]
    dot_general x2 -> x0, local copies, waits for them, and re-layouts: 3.08 us -> none  [the longest x1 1.89 us: body(): jnp.einsum('kic,kjc->ijc', matching, lax.all_gather(right, 'row', axis=0,...]
  transfers between devices with their start and end apart: 8 -> 0, of which waited for: 6 -> 0; matrix products, arithmetic and copies ran while one was open for 2% -> 0% of each run, Pallas kernels for 0% -> 0%
where the time goes in v2:
time: 42.2 us; the launch traced here: 41.9 us
  Pallas kernels  40.2 us (95%)
  local copies, waits for them, and re-layouts  1.69 us (4%)
    pallas_call x1, Pallas kernels, body(): pl.pallas_call(functools.partial(kernel, n, size), out_shape=jax.ShapeDty...  40.2 us
    unnamed x1, local copies, waits for them, and re-layouts  1.69 us

profile of v2, /device:TPU:0, one launch (start us, length us, event | category | flops | bytes accessed | tf_op | source)
XLA Modules:
  0.0 41.9 jit_solution(13086325325432026482)
XLA Ops:
  0.0 40.2 %shard_map.73 = f32[24,24,128]{2,1,0:T(8,128)} custom-call(f32[24,24,128]{2,1,0:T(8,128)} %pair_hbm.1, s32[24,24]{1,0:T(8,128)} %mask_hbm.1, s32[96]{0:T(128)} %chain_hbm.1, f32[2,128]{1,0:T(2,128)} %table_hbm.1, f32[2,4,128]{2,1,0:T(4,128)} %norms_hbm.1, bf16[2,128,640]{2,1,0:T(8,128)(2,1)} %w_in_hbm.1, bf16[2,128,128]{2,1,0:T(8,128)(2,1)} %w_out_hbm.1), custom_call_target="tpu_custom_call" | custom-call | tf_op jit(solution)/shard_map/pallas_call | solution.py:330
  40.2 1.7 %copy.9 = f32[24,24,128]{2,1,0:T(8,128)} copy(f32[24,24,128]{2,1,0:T(8,128)} %shard_map.73) | data formatting | bytes 589824

commit v3 on v2

--- a/solution.py
+++ b/solution.py
@@ -57,6 +57,7 @@
     operand,
     triangle,
     total,
+    kept,
     right_slots,
     left_slots,
     part_one,
@@ -129,9 +130,19 @@
         return copy(right_slots, 0, right_slots, s, q, send_right, recv_right, along_row(s))
 
     def left_copy(q, s):
+        if s > 1 and s % 2 == 1:
+            return copy(
+                left_slots, s - 1, left_slots, s, q, send_left, recv_left, along_col(1)
+            )
         return copy(left_slots, 0, left_slots, s, q, send_left, recv_left, along_col(s))
 
-    def one_copy(q, s):
+    def landed(q, s):
+        return copy(left_slots, 0, left_slots, s, q, send_left, recv_left, along_col(1))
+
+    def near_copy(q, s):
+        return copy(part_one, s, got_one, s, q, send_one, recv_one, along_col(1))
+
+    def far_copy(q, s):
         return copy(part_one, s, got_one, s, q, send_one, recv_one, along_col(s))
 
     def two_copy(q, s):
@@ -222,41 +233,63 @@
             def _():
                 total[at(q), :] = triangle[...]
 
-            @pl.when(slot > 0)
+            @pl.when(slot % 2 == 1)
             def _():
                 part_one[slot, at(q), :] = triangle[...].astype(BF16)
-                one_copy(q, slot).start()
+                near_copy(q, slot).start()
+
+            @pl.when(jnp.logical_and(slot > 0, slot % 2 == 0))
+            def _():
+                kept[slot // 2, at(q), :] = triangle[...]
 
             return carry
 
         lax.fori_loop(0, n, step, 0)
 
+    def combine(q):
+        for s in range(2, n, 2):
+            near_copy(q, s + 1).wait_recv()
+            both = kept[s // 2, at(q), :] + got_one[s + 1, at(q), :].astype(F32)
+            part_one[s, at(q), :] = both.astype(BF16)
+            far_copy(q, s).start()
+
+    def forward(q):
+        for s in range(2, n, 2):
+            left_copy(q, s).wait_recv()
+            left_copy(q, s + 1).start()
+
     def between(q):
-        for s in range(1, n):
-            one_copy(q, s).wait_recv()
-        whole = total[at(q), :]
-        for s in range(1, n):
+        near_copy(q, 1).wait_recv()
+        whole = total[at(q), :] + got_one[1, at(q), :].astype(F32)
+        for s in range(2, n, 2):
+            far_copy(q, s).wait_recv()
             whole = whole + got_one[s, at(q), :].astype(F32)
         total[at(q), :] = whole
         state[at(q), :] = updated(0, at(q))
         norm(1, q)
         left_slots[0, at(q), :] = value_of(1, q, 0).astype(BF16)
-        for s in range(1, n):
+        for s in [1] + list(range(2, n, 2)):
             left_copy(q, s).start()
         own_right[at(q), :] = value_of(1, q, 2).astype(BF16).astype(F32)
         gate_of(1, q)
 
-    for q in range(count):
+    outgoing(0)
+    for q in range(1, count):
         outgoing(q)
+        combine(q - 1)
+        if q > 1:
+            between(q - 2)
+    combine(count - 1)
+    for q in range(max(count - 2, 0), count):
+        between(q)
         if q > 0:
-            between(q - 1)
-    between(count - 1)
+            forward(q - 1)
 
     def incoming(q):
         def step(s, carry):
-            @pl.when(s > 0)
-            def _():
-                left_copy(q, s).wait_recv()
+            @pl.when(s % 2 == 1)
+            def _():
+                landed(q, s).wait_recv()
 
             operand[...] = left_slots[s, at(q), :].astype(F32)
             sums = [[jnp.zeros((LINES, width), F32) for _ in range(LINES)] for _ in range(count)]
@@ -303,13 +336,15 @@
 
     for q in range(count):
         incoming(q)
-        if q > 0:
+        if q == 0:
+            forward(count - 1)
+        else:
             last(q - 1)
     last(count - 1)
     for q in range(count):
         for s in range(1, n):
             right_copy(q, s).wait_send()
-            one_copy(q, s).wait_send()
+            near_copy(q, s).wait_send()
             left_copy(q, s).wait_send()
             two_copy(q, s).wait_send()
 
@@ -337,6 +372,7 @@
         + [flat] * 5
         + [few] * 2
         + [flat]
+        + [pltpu.VMEM((max(n // 2, 1), rows, width), F32)]
         + [slots] * 6
         + [pltpu.SemaphoreType.DMA((len(inputs),))]
         + [pltpu.SemaphoreType.DMA((size // LINES, n))] * 8,

time: 42.2 us -> 39 us (0.924)
  Pallas kernels: 40.2 us -> 37.1 us
    pallas_call x1, Pallas kernels: 40.2 us -> 37.1 us  [body(): pl.pallas_call(functools.partial(kernel, n, size), out_shape=jax.ShapeDty...]
where the time goes in v3:
time: 39 us; the launch traced here: 38.8 us
  Pallas kernels  37.1 us (95%)
  local copies, waits for them, and re-layouts  1.69 us (4%)
    pallas_call x1, Pallas kernels, body(): pl.pallas_call(functools.partial(kernel, n, size), out_shape=jax.ShapeDty...  37.1 us
    unnamed x1, local copies, waits for them, and re-layouts  1.69 us

profile of v3, /device:TPU:0, one launch (start us, length us, event | category | flops | bytes accessed | tf_op | source)
XLA Modules:
  0.0 38.8 jit_solution(17098238116195294247)
XLA Ops:
  0.0 37.1 %shard_map.73 = f32[24,24,128]{2,1,0:T(8,128)} custom-call(f32[24,24,128]{2,1,0:T(8,128)} %pair_hbm.1, s32[24,24]{1,0:T(8,128)} %mask_hbm.1, s32[96]{0:T(128)} %chain_hbm.1, f32[2,128]{1,0:T(2,128)} %table_hbm.1, f32[2,4,128]{2,1,0:T(4,128)} %norms_hbm.1, bf16[2,128,640]{2,1,0:T(8,128)(2,1)} %w_in_hbm.1, bf16[2,128,128]{2,1,0:T(8,128)(2,1)} %w_out_hbm.1), custom_call_target="tpu_custom_call" | custom-call | tf_op jit(solution)/shard_map/pallas_call | solution.py:365
  37.1 1.7 %copy.9 = f32[24,24,128]{2,1,0:T(8,128)} copy(f32[24,24,128]{2,1,0:T(8,128)} %shard_map.73) | data formatting | bytes 589824
